TPU v7x, 32 devices: a whole 2x2x4 slice. The times are simulated.
32 devices in a mesh: blk: 8 (over y, x, core), sub: 4 (over z).
Axes of the slice: x: 2, y: 2, z: 4, core: 2. Of those that a mesh axis runs over, the one named last changes fastest.
Arguments:
- user_factors: float32 [32768, 1024], P(('blk', 'sub')), may hold values from -6 to 6
- item_factors: bfloat16 [2048, 1024], P(('blk', 'sub')), may hold values from -6 to 6
- ratings: bfloat16 [32768, 1024], P(('blk', 'sub')), may hold values from -6 to 6
- presence: int32 [256, 8, 2], P(('blk', 'sub')), may hold values 0 or 1
- visit_order: int32 [8], replicated, may hold values from 0 to 7, each once
Outputs:
- users_out: float32 [32768, 1024], P(('blk', 'sub'))
- items_out: bfloat16 [2048, 1024], P(('blk', 'sub'))
All inputs are finite; a program needn't handle non-finite values. No bound on the sum of `presence` on one device may be relied on, other than what follows from the above.
Results may differ from a plain program's by a relative error of at most 0.017.
Values may be sent and summed in bfloat16 or wider, within the bound.
A program may use at most 64 MiB of HBM per device.

v0:
```python
import math

import jax
import jax.numpy as jnp
from jax import lax
from jax.sharding import PartitionSpec as P

R = 1024
BS = 256
TICKS = 4


learn_users = 0.5
decay_weight = 0.05


def passed_along(block, axis, distance):
    devices = range(lax.axis_size(axis))
    route = [((i - distance) % len(devices), i) for i in devices]
    return lax.ppermute(block, axis, route)


def on_device(user_factors, item_factors, ratings, presence, visit_order):
    scale = R ** (-0.5)
    group_count = lax.axis_size("blk")
    group = lax.axis_index("blk")
    part_index = lax.axis_index("sub")
    part_rows = item_factors.shape[0]
    local_users = user_factors.shape[0]
    group_users = lax.axis_size("sub") * local_users
    step_items = 0.9 * R / (math.sqrt(group_users) + math.sqrt(R)) ** 2
    tile_users = presence.shape[0]
    tile_items = presence.shape[2]
    users_now = user_factors
    held_part = item_factors
    for step_index in range(TICKS):
        item_block = lax.all_gather(held_part, "sub", axis=0, tiled=True)
        position = jnp.mod(group - step_index, group_count)
        ident = jnp.sum(jnp.where(jnp.arange(group_count) == position, visit_order, 0))
        picked = lax.dynamic_index_in_dim(presence, ident, 1, keepdims=False)
        present = jnp.broadcast_to(
            picked[:, None, :, None],
            (tile_users, local_users // tile_users, tile_items, BS // tile_items),
        )
        present = present.reshape(local_users, BS).astype(jnp.float32)
        users_half = users_now.astype(jnp.bfloat16)
        predicted = (
            lax.dot_general(
                users_half, item_block, (((1,), (1,)), ((), ())), preferred_element_type=jnp.float32
            )
            * scale
        )
        targets = ratings[:, step_index * BS : (step_index + 1) * BS].astype(jnp.float32)
        residual = (present * (predicted - targets)).astype(jnp.bfloat16)
        user_grad = jnp.dot(residual, item_block, preferred_element_type=jnp.float32) * scale
        item_part = (
            lax.dot_general(
                residual, users_half, (((0,), (0,)), ((), ())), preferred_element_type=jnp.float32
            )
            * scale
        ).astype(jnp.bfloat16)
        users_now = users_now - learn_users * (user_grad + decay_weight * users_now)
        item_grad = lax.psum_scatter(item_part, "sub", scatter_dimension=0, tiled=True).astype(
            jnp.float32
        )
        own_rows = lax.dynamic_slice_in_dim(
            item_block, part_index * part_rows, part_rows, 0
        ).astype(jnp.float32)
        updated = (own_rows - step_items * (item_grad + decay_weight * own_rows)).astype(
            jnp.bfloat16
        )
        held_part = passed_along(updated, "blk", 1)
    return (users_now, held_part)


def solution(mesh):
    in_specs = (
        P(("blk", "sub"), None),
        P(("blk", "sub"), None),
        P(("blk", "sub"), None),
        P(("blk", "sub"), None, None),
        P(),
    )
    out_specs = (P(("blk", "sub"), None), P(("blk", "sub"), None))
    return jax.shard_map(
        on_device, mesh=mesh, in_specs=in_specs, out_specs=out_specs, check_vma=False
    )
```

profile of v0, /device:TPU:1, one launch (start us, length us, event | category | flops | bytes accessed | tf_op | source)
XLA Modules:
  0.0 212.0 jit_solution(3343628173618602564)
XLA Ops:
  7.2 0.0 reduce-scatter.5.cloned.1.call-start
  7.3 1.4 fusion.39
  16.3 0.9 constant_dynamic-slice_fusion
  17.3 0.1 copy.23
  17.4 0.1 copy.16
  17.4 0.0 copy-start.3
  17.4 15.6 %all_gather.12 = bf16[256,1024]{1,0:T(8,128)(2,1)S(1)} all-gather(bf16[64,1024]{1,0:T(8,128)(2,1)} %param.6), channel_id=1, replica_groups=mesh['blk'=8,'sub'=4] {'sub'}, dimensions={0}, use_global_device_ids=true | all-gather | bytes 655360 | tf_op jit(solution)/shard_map/all_gather | solution.py:37
  33.1 0.3 broadcast_in_dim.16
  33.4 3.1 %fusion.8 = bf16[1024,256]{1,0:T(8,128)(2,1)S(1)} fusion(bf16[256,1024]{1,0:T(8,128)(2,1)S(1)} %all_gather.12, f32[128,8,2,128]{3,2,1,0:T(2,128)S(1)} %bitcast.40, f32[1024,1024]{1,0:T(8,128)} %param.5, bf16[1024,1024]{1,0:T(8,128)(2,1)} %param.7), kind=kOutput, calls=%fused_computation.20 | convolution fusion | flops 539230208 | bytes 6815744 | tf_op jit(solution)/shard_map/dot_general | solution.py:48
  36.5 0.0 copy-done.3
  36.5 1.5 fusion.9
  38.0 0.0 reduce-scatter.5.cloned.1.call-update
  38.1 0.0 reduce-scatter.7.cloned.1.call-start
  38.1 0.1 copy.24
  38.2 0.0 copy-start.4
  38.2 5.3 %multiply_subtract_fusion.3 = f32[1024,1024]{1,0:T(8,128)} fusion(f32[1024,1024]{1,0:T(8,128)} %param.5, bf16[1024,256]{1,0:T(8,128)(2,1)S(1)} %fusion.8, bf16[256,1024]{1,0:T(8,128)(2,1)S(1)} %all_gather.12), kind=kOutput, calls=%fused_computation.3 | convolution fusion | flops 542113792 | bytes 9437184 | tf_op jit(solution)/shard_map/dot_general | solution.py:55
  43.5 17.7 %reduce-scatter.5.cloned.1.call-done = bf16[64,1024]{1,0:T(8,128)(2,1)} async-done(((bf16[256,1024]{1,0:T(8,128)(2,1)}), bf16[64,1024]{1,0:T(8,128)(2,1)}) %reduce-scatter.5.cloned.1.call-update) | async-done | bytes 131088 | tf_op jit(solution)/shard_map/reduce_scatter | solution.py:63
  61.2 1.0 fusion.26
  62.1 3.7 %collective-permute-start = (bf16[64,1024]{1,0:T(8,128)(2,1)S(1)}, bf16[64,1024]{1,0:T(8,128)(2,1)S(1)}, u32[]{:S(2)}, u32[]{:S(2)}) collective-permute-start(bf16[64,1024]{1,0:T(8,128)(2,1)S(1)} %fusion.26), channel_id=1, source_target_pairs={{28,0},{0,4},{4,8},{8,12},{12,16},{16,20},{20,24},{24,28},{29,1},{... | collective-permute-start | bytes 393224 | tf_op jit(solution)/shard_map/ppermute | solution.py:20
  65.8 0.1 copy.18
  65.9 1.9 collective-permute-done
  67.7 12.5 %all_gather.13 = bf16[256,1024]{1,0:T(8,128)(2,1)S(1)} all-gather(bf16[64,1024]{1,0:T(8,128)(2,1)S(1)} %collective-permute-done), channel_id=1, replica_groups=mesh['blk'=8,'sub'=4] {'sub'}, dimensions={0}, use_global_device_ids=true | all-gather | bytes 655360 | tf_op jit(solution)/shard_map/all_gather | solution.py:37
  80.3 0.3 broadcast_in_dim.17
  80.6 0.0 copy-done.4
  80.6 3.0 %fusion.10 = bf16[1024,256]{1,0:T(8,128)(2,1)S(1)} fusion(bf16[256,1024]{1,0:T(8,128)(2,1)S(1)} %all_gather.13, f32[128,8,2,128]{3,2,1,0:T(2,128)S(1)} %bitcast.41, f32[1024,1024]{1,0:T(8,128)} %multiply_subtract_fusion.3, bf16[1024,1024]{1,0:T(8,128)(2,1)S(1)} %copy-done.4), kind=kOutput, calls=%fused_computation.22 | convolution fusion | flops 539230208 | bytes 6815744 | tf_op jit(solution)/shard_map/dot_general | solution.py:48
  83.6 0.0 copy-done
  83.6 1.5 fusion.11
  85.1 0.0 reduce-scatter.7.cloned.1.call-update
  85.1 0.0 reduce-scatter.9.cloned.1.call-start
  85.2 0.1 copy.25
  85.3 0.1 copy.20
  85.4 21.7 %reduce-scatter.7.cloned.1.call-done = bf16[64,1024]{1,0:T(8,128)(2,1)} async-done(((bf16[256,1024]{1,0:T(8,128)(2,1)}), bf16[64,1024]{1,0:T(8,128)(2,1)}) %reduce-scatter.7.cloned.1.call-update) | async-done | bytes 131088 | tf_op jit(solution)/shard_map/reduce_scatter | solution.py:63
  107.0 1.0 fusion.29
  108.0 3.6 %collective-permute-start.1 = (bf16[64,1024]{1,0:T(8,128)(2,1)S(1)}, bf16[64,1024]{1,0:T(8,128)(2,1)S(1)}, u32[]{:S(2)}, u32[]{:S(2)}) collective-permute-start(bf16[64,1024]{1,0:T(8,128)(2,1)S(1)} %fusion.29), channel_id=1, source_target_pairs={{28,0},{0,4},{4,8},{8,12},{12,16},{16,20},{20,24},{24,28},{29,1},{... | collective-permute-start | bytes 393224 | tf_op jit(solution)/shard_map/ppermute | solution.py:20
  111.6 3.1 %multiply_subtract_fusion.2 = f32[1024,1024]{1,0:T(8,128)S(1)} fusion(f32[1024,1024]{1,0:T(8,128)} %multiply_subtract_fusion.3, bf16[1024,256]{1,0:T(8,128)(2,1)S(1)} %fusion.10, bf16[256,1024]{1,0:T(8,128)(2,1)S(1)} %all_gather.13), kind=kOutput, calls=%fused_computation.2 | convolution fusion | flops 542113792 | bytes 9437184 | tf_op jit(solution)/shard_map/dot_general | solution.py:55
  114.7 0.0 copy-start.1
  114.7 0.0 collective-permute-done.1
  114.7 12.0 %all_gather.14 = bf16[256,1024]{1,0:T(8,128)(2,1)S(1)} all-gather(bf16[64,1024]{1,0:T(8,128)(2,1)S(1)} %collective-permute-done.1), channel_id=1, replica_groups=mesh['blk'=8,'sub'=4] {'sub'}, dimensions={0}, use_global_device_ids=true | all-gather | bytes 655360 | tf_op jit(solution)/shard_map/all_gather | solution.py:37
  126.7 0.3 broadcast_in_dim.34
  127.0 0.8 fusion.12
  127.8 0.0 copy-done.1
  127.8 1.5 fusion.13
  129.4 0.0 reduce-scatter.9.cloned.1.call-update
  129.4 0.0 reduce-scatter.11.cloned.1.call-start
  129.4 0.1 copy.26
  129.5 0.1 copy.22
  129.6 21.5 %reduce-scatter.9.cloned.1.call-done = bf16[64,1024]{1,0:T(8,128)(2,1)} async-done(((bf16[256,1024]{1,0:T(8,128)(2,1)}), bf16[64,1024]{1,0:T(8,128)(2,1)}) %reduce-scatter.9.cloned.1.call-update) | async-done | bytes 131088 | tf_op jit(solution)/shard_map/reduce_scatter | solution.py:63
  151.1 1.0 fusion.32
  152.1 3.5 %collective-permute-start.2 = (bf16[64,1024]{1,0:T(8,128)(2,1)S(1)}, bf16[64,1024]{1,0:T(8,128)(2,1)S(1)}, u32[]{:S(2)}, u32[]{:S(2)}) collective-permute-start(bf16[64,1024]{1,0:T(8,128)(2,1)S(1)} %fusion.32), channel_id=1, source_target_pairs={{28,0},{0,4},{4,8},{8,12},{12,16},{16,20},{20,24},{24,28},{29,1},{... | collective-permute-start | bytes 393224 | tf_op jit(solution)/shard_map/ppermute | solution.py:20
  155.6 3.1 %multiply_subtract_fusion.1 = f32[1024,1024]{1,0:T(8,128)S(1)} fusion(f32[1024,1024]{1,0:T(8,128)} %copy-done.1, bf16[1024,256]{1,0:T(8,128)(2,1)S(1)} %fusion.12, bf16[256,1024]{1,0:T(8,128)(2,1)S(1)} %all_gather.14), kind=kOutput, calls=%fused_computation.1 | convolution fusion | flops 542113792 | bytes 9437184 | tf_op jit(solution)/shard_map/dot_general | solution.py:55
  158.7 0.0 copy-start.2
  158.7 0.0 collective-permute-done.2
  158.7 11.9 %all_gather.15 = bf16[256,1024]{1,0:T(8,128)(2,1)S(1)} all-gather(bf16[64,1024]{1,0:T(8,128)(2,1)S(1)} %collective-permute-done.2), channel_id=1, replica_groups=mesh['blk'=8,'sub'=4] {'sub'}, dimensions={0}, use_global_device_ids=true | all-gather | bytes 655360 | tf_op jit(solution)/shard_map/all_gather | solution.py:37
  170.6 0.3 broadcast_in_dim.35
  171.0 0.8 fusion.14
  171.8 0.0 copy-done.2
  171.8 1.5 fusion.15
  173.3 0.0 reduce-scatter.11.cloned.1.call-update
  173.3 21.9 %reduce-scatter.11.cloned.1.call-done = bf16[64,1024]{1,0:T(8,128)(2,1)} async-done(((bf16[256,1024]{1,0:T(8,128)(2,1)}), bf16[64,1024]{1,0:T(8,128)(2,1)}) %reduce-scatter.11.cloned.1.call-update) | async-done | bytes 131088 | tf_op jit(solution)/shard_map/reduce_scatter | solution.py:63
  195.3 1.0 fusion.35
  196.3 3.5 %collective-permute-start.3 = (bf16[64,1024]{1,0:T(8,128)(2,1)S(1)}, bf16[64,1024]{1,0:T(8,128)(2,1)S(1)}, u32[]{:S(2)}, u32[]{:S(2)}) collective-permute-start(bf16[64,1024]{1,0:T(8,128)(2,1)S(1)} %fusion.35), channel_id=1, source_target_pairs={{28,0},{0,4},{4,8},{8,12},{12,16},{16,20},{20,24},{24,28},{29,1},{... | collective-permute-start | bytes 393224 | tf_op jit(solution)/shard_map/ppermute | solution.py:20
  199.7 5.1 %multiply_subtract_fusion = f32[1024,1024]{1,0:T(8,128)} fusion(f32[1024,1024]{1,0:T(8,128)} %copy-done.2, bf16[1024,256]{1,0:T(8,128)(2,1)S(1)} %fusion.14, bf16[256,1024]{1,0:T(8,128)(2,1)S(1)} %all_gather.15), kind=kOutput, calls=%fused_computation | convolution fusion | flops 542113792 | bytes 9437184 | tf_op jit(solution)/shard_map/dot_general | solution.py:55
  204.8 0.0 collective-permute-done.3
  204.8 0.7 copy.36
  (5 shorter events, 0.0 us)
Async XLA Ops:
  7.2 54.0 %reduce-scatter.5.cloned.1.call-start = ((), (), s32[]{:S(2)}) async-start(), calls=%async_computation.4 | async-start | bytes 655360 | tf_op jit(solution)/shard_map/reduce_scatter | solution.py:63
  17.4 19.1 %copy-start.3 = (f32[1024,1024]{1,0:T(8,128)S(1)}, f32[1024,1024]{1,0:T(8,128)}, u32[]{:S(2)}) copy-start(f32[1024,1024]{1,0:T(8,128)} %param.5) | copy-start | bytes 12582916
  38.1 69.0 %reduce-scatter.7.cloned.1.call-start = ((), (), s32[]{:S(2)}) async-start(), calls=%async_computation.5 | async-start | bytes 655360 | tf_op jit(solution)/shard_map/reduce_scatter | solution.py:63
  38.2 42.4 %copy-start.4 = (bf16[1024,1024]{1,0:T(8,128)(2,1)S(1)}, bf16[1024,1024]{1,0:T(8,128)(2,1)}, u32[]{:S(2)}) copy-start(bf16[1024,1024]{1,0:T(8,128)(2,1)} %param.7) | copy-start | bytes 6291460
  62.1 5.6 %collective-permute-start = (bf16[64,1024]{1,0:T(8,128)(2,1)S(1)}, bf16[64,1024]{1,0:T(8,128)(2,1)S(1)}, u32[]{:S(2)}, u32[]{:S(2)}) collective-permute-start(bf16[64,1024]{1,0:T(8,128)(2,1)S(1)} %fusion.26), channel_id=1, source_target_pairs={{28,0},{0,4},{4,8},{8,12},{12,16},{16,20},{20,24},{24,28},{29,1},{... | collective-permute-start | bytes 393224 | tf_op jit(solution)/shard_map/ppermute | solution.py:20
  65.9 17.7 %copy-start = (f32[1024,1024]{1,0:T(8,128)S(1)}, f32[1024,1024]{1,0:T(8,128)}, u32[]{:S(2)}) copy-start(f32[1024,1024]{1,0:T(8,128)} %multiply_subtract_fusion.3) | copy-start | bytes 12582916
  85.1 66.0 %reduce-scatter.9.cloned.1.call-start = ((), (), s32[]{:S(2)}) async-start(), calls=%async_computation.6 | async-start | bytes 655360 | tf_op jit(solution)/shard_map/reduce_scatter | solution.py:63
  108.0 6.7 %collective-permute-start.1 = (bf16[64,1024]{1,0:T(8,128)(2,1)S(1)}, bf16[64,1024]{1,0:T(8,128)(2,1)S(1)}, u32[]{:S(2)}, u32[]{:S(2)}) collective-permute-start(bf16[64,1024]{1,0:T(8,128)(2,1)S(1)} %fusion.29), channel_id=1, source_target_pairs={{28,0},{0,4},{4,8},{8,12},{12,16},{16,20},{20,24},{24,28},{29,1},{... | collective-permute-start | bytes 393224 | tf_op jit(solution)/shard_map/ppermute | solution.py:20
  114.7 13.1 %copy-start.1 = (f32[1024,1024]{1,0:T(8,128)}, f32[1024,1024]{1,0:T(8,128)S(1)}, u32[]{:S(2)}) copy-start(f32[1024,1024]{1,0:T(8,128)S(1)} %multiply_subtract_fusion.2) | copy-start | bytes 12582916
  129.4 65.9 %reduce-scatter.11.cloned.1.call-start = ((), (), s32[]{:S(2)}) async-start(), calls=%async_computation.7 | async-start | bytes 655360 | tf_op jit(solution)/shard_map/reduce_scatter | solution.py:63
  152.1 6.6 %collective-permute-start.2 = (bf16[64,1024]{1,0:T(8,128)(2,1)S(1)}, bf16[64,1024]{1,0:T(8,128)(2,1)S(1)}, u32[]{:S(2)}, u32[]{:S(2)}) collective-permute-start(bf16[64,1024]{1,0:T(8,128)(2,1)S(1)} %fusion.32), channel_id=1, source_target_pairs={{28,0},{0,4},{4,8},{8,12},{12,16},{16,20},{20,24},{24,28},{29,1},{... | collective-permute-start | bytes 393224 | tf_op jit(solution)/shard_map/ppermute | solution.py:20
  158.7 13.1 %copy-start.2 = (f32[1024,1024]{1,0:T(8,128)}, f32[1024,1024]{1,0:T(8,128)S(1)}, u32[]{:S(2)}) copy-start(f32[1024,1024]{1,0:T(8,128)S(1)} %multiply_subtract_fusion.1) | copy-start | bytes 12582916
  196.3 8.6 %collective-permute-start.3 = (bf16[64,1024]{1,0:T(8,128)(2,1)S(1)}, bf16[64,1024]{1,0:T(8,128)(2,1)S(1)}, u32[]{:S(2)}, u32[]{:S(2)}) collective-permute-start(bf16[64,1024]{1,0:T(8,128)(2,1)S(1)} %fusion.35), channel_id=1, source_target_pairs={{28,0},{0,4},{4,8},{8,12},{12,16},{16,20},{20,24},{24,28},{29,1},{... | collective-permute-start | bytes 393224 | tf_op jit(solution)/shard_map/ppermute | solution.py:20
Sparse Core Ops, SparseCore 0:
  38.2 22.9 reduce-scatter.4
  85.3 21.7 reduce-scatter.6
  129.5 21.5 reduce-scatter.8
  173.5 21.7 reduce-scatter.10
where the time goes:
time: 213 us; the launch traced here: 212 us
  waiting for transfers between devices  84.7 us (40%)
  blocking collectives  52.1 us (24%)
  matrix products  30.3 us (14%)
  between operations  21.6 us (10%)
  starting transfers between devices  14.3 us (7%)
  other arithmetic  5.3 us (2%)
  local copies, waits for them, and re-layouts  3.67 us (2%)
    reduce_scatter x4, waiting for transfers between devices, on_device(): lax.psum_scatter(item_part, 'sub', scatter_dimension=0, tiled=True)  82.8 us
    all_gather x4, blocking collectives, on_device(): item_block = lax.all_gather(held_part, 'sub', axis=0, tiled=True)  52.1 us
    dot_general x4, matrix products, on_device(): jnp.dot(residual, item_block, preferred_element_type=jnp.float32) * scale  16.6 us
    ppermute x4, starting transfers between devices, passed_along(): return lax.ppermute(block, axis, route)  14.2 us
    dot_general x4, matrix products, on_device(): lax.dot_general(users_half, item_block, (((1,), (1,)), ((), ())), preferr...  7.6 us
    dot_general x4, matrix products, on_device(): lax.dot_general(residual, users_half, (((0,), (0,)), ((), ())), preferred...  6.13 us
  transfers between devices with their start and end apart: 8, of which 5 were waited for; matrix products, arithmetic and copies ran while one was open for 8% of the time, Pallas kernels for 0%

commit v1 on v0

--- a/solution.py
+++ b/solution.py
@@ -1,14 +1,17 @@
+import functools
 import math
 
 import jax
 import jax.numpy as jnp
 from jax import lax
+from jax.experimental import pallas as pl
+from jax.experimental.pallas import tpu as pltpu
 from jax.sharding import PartitionSpec as P
 
 R = 1024
 BS = 256
 TICKS = 4
-
+MESH = pl.DeviceIdType.MESH
 
 learn_users = 0.5
 decay_weight = 0.05
@@ -20,15 +23,18 @@
     return lax.ppermute(block, axis, route)
 
 
-def on_device(user_factors, item_factors, ratings, presence, visit_order):
+def step_size(group_users):
+    return 0.9 * R / (math.sqrt(group_users) + math.sqrt(R)) ** 2
+
+
+def by_collectives(user_factors, item_factors, ratings, presence, visit_order):
     scale = R ** (-0.5)
     group_count = lax.axis_size("blk")
     group = lax.axis_index("blk")
     part_index = lax.axis_index("sub")
     part_rows = item_factors.shape[0]
     local_users = user_factors.shape[0]
-    group_users = lax.axis_size("sub") * local_users
-    step_items = 0.9 * R / (math.sqrt(group_users) + math.sqrt(R)) ** 2
+    step_items = step_size(lax.axis_size("sub") * local_users)
     tile_users = presence.shape[0]
     tile_items = presence.shape[2]
     users_now = user_factors
@@ -73,6 +79,299 @@
     return (users_now, held_part)
 
 
+LINE = 4
+CHUNKS = 2
+HALVES = 2
+
+
+def line_kernel(
+    n_blk, step_items,
+    users_hbm, items_hbm, ratings_hbm, presence_ref, order_ref,
+    users_out, items_out,
+    users, items, users_half, ratings, targets, res, res_t, first_sum, blk, part, sent, upd, final,
+    local_sem, gather_send, gather_recv, part_send, part_recv,
+    final_send, final_recv,
+):
+    scale = R ** (-0.5)
+    g, s = lax.axis_index("blk"), lax.axis_index("sub")
+    onward, back = lax.rem(g + 1, n_blk), lax.rem(g + n_blk - 1, n_blk)
+    n_users = users.shape[0]
+    rows = items.shape[0] // CHUNKS
+    size = LINE * rows
+    wide = R // HALVES
+    tile_users, tile_items = presence_ref.shape[0], presence_ref.shape[1]
+    tile_rows = n_users // tile_users
+
+    def remote(src, dst, send, recv, device):
+        return pltpu.make_async_remote_copy(
+            src_ref=src, dst_ref=dst, send_sem=send, recv_sem=recv,
+            device_id=device, device_id_type=MESH,
+        )
+
+    def some(first, count=1):
+        return pl.ds(pl.multiple_of(first * rows, rows), count * rows)
+
+    def columns(h):
+        return pl.ds(h * wide, wide)
+
+    load_items = pltpu.make_async_copy(items_hbm, items, local_sem.at[0])
+    load_users = pltpu.make_async_copy(users_hbm, users, local_sem.at[1])
+    load_ratings = pltpu.make_async_copy(ratings_hbm, ratings, local_sem.at[2])
+    load_items.start()
+    load_users.start()
+    load_ratings.start()
+
+    barrier = pltpu.get_barrier_semaphore()
+    for k in range(1, LINE):
+        pl.semaphore_signal(
+            barrier, inc=1, device_id=(g, lax.rem(s + k, LINE)), device_id_type=MESH
+        )
+    for group in (onward, back):
+        for k in range(LINE):
+            pl.semaphore_signal(barrier, inc=1, device_id=(group, k), device_id_type=MESH)
+    pl.semaphore_wait(barrier, 3 * LINE - 1)
+
+    def chunk_rows(c, j, count=1):
+        return pl.ds(pl.multiple_of(c * size + j * rows, rows), count * rows)
+
+    def first_copies(c, h):
+        src = items.at[pl.ds(c * rows, rows), columns(h)]
+        return [
+            remote(src, blk.at[0, chunk_rows(c, s), columns(h)], gather_send.at[0, c, h, k],
+                   gather_recv.at[0, c, h], (g, lax.rem(s + 1 + k, LINE)))
+            for k in range(LINE - 1)
+        ]
+
+    def gather_copies(t, c, h):
+        return [
+            remote(upd.at[t, c, h], blk.at[t + 1, chunk_rows(c, s), columns(h)],
+                   gather_send.at[t + 1, c, h, k], gather_recv.at[t + 1, c, h],
+                   (onward, lax.rem(s + k, LINE)))
+            for k in range(LINE)
+        ]
+
+    def arrival(t, c, h):
+        count = LINE - 1 if t == 0 else LINE
+        ref = blk.at[t, pl.ds(c * size, count * rows), columns(h)]
+        return remote(ref, ref, gather_send.at[t, c, h, 0], gather_recv.at[t, c, h],
+                      (g, lax.rem(s + 1, LINE)))
+
+    def part_copies(t, c, h):
+        return [
+            remote(part.at[t, c, h, some(lax.rem(s + k, LINE)), :], sent.at[t, c, h, k - 1],
+                   part_send.at[t, c, h, k - 1], part_recv.at[t, c, h],
+                   (g, lax.rem(s + k, LINE)))
+            for k in range(1, LINE)
+        ]
+
+    def part_arrival(t, c, h):
+        return remote(sent.at[t, c, h], sent.at[t, c, h], part_send.at[t, c, h, 0],
+                      part_recv.at[t, c, h], (g, lax.rem(s + 1, LINE)))
+
+    def final_copy(c, h):
+        return remote(upd.at[TICKS - 1, c, h], final.at[pl.ds(c * rows, rows), columns(h)],
+                      final_send.at[c, h], final_recv.at[c, h], (onward, s))
+
+    load_items.wait()
+    for c in range(CHUNKS):
+        for h in range(HALVES):
+            for copy in first_copies(c, h):
+                copy.start()
+        blk[0, chunk_rows(c, s), :] = items[c * rows : (c + 1) * rows, :]
+
+    load_ratings.wait()
+    for t in range(TICKS):
+        for c in range(CHUNKS):
+            for k in range(LINE):
+                begin = t * BS + (k * CHUNKS + c) * rows
+                targets[t, :, c * size + k * rows : c * size + (k + 1) * rows] = ratings[
+                    :, begin : begin + rows
+                ]
+    load_users.wait()
+    tall = min(256, n_users)
+
+    def round_users(i, carry):
+        at_rows = pl.ds(pl.multiple_of(i * tall, tall), tall)
+        users_half[at_rows, :] = users[at_rows, :].astype(jnp.bfloat16)
+        return carry
+
+    lax.fori_loop(0, n_users // tall, round_users, 0)
+
+    def work(t, c):
+        ident = order_ref[0, lax.rem(g + n_blk - t % n_blk, n_blk)]
+        column = lax.broadcasted_iota(jnp.int32, (1, size), 1)
+        row_of = (column // rows) * (CHUNKS * rows) + c * rows + column % rows
+        tile_of = row_of // (BS // tile_items)
+        step_rows = 4 * tile_rows
+
+        def product(at_rows, h):
+            part_columns = slice(h * wide, (h + 1) * wide)
+            return lax.dot_general(
+                users_half[at_rows, part_columns],
+                blk[t, c * size : (c + 1) * size, part_columns],
+                (((1,), (1,)), ((), ())), preferred_element_type=jnp.float32,
+            )
+
+        for h in range(HALVES - 1):
+            arrival(t, c, h).wait_recv()
+
+            def add(i, carry):
+                at_rows = pl.ds(pl.multiple_of(i * step_rows, step_rows), step_rows)
+                if h == 0:
+                    first_sum[at_rows, :] = product(at_rows, h)
+                else:
+                    first_sum[at_rows, :] += product(at_rows, h)
+                return carry
+
+            lax.fori_loop(0, n_users // step_rows, add, 0, unroll=True)
+        arrival(t, c, HALVES - 1).wait_recv()
+
+        def predict(i, carry):
+            at_rows = pl.ds(pl.multiple_of(i * step_rows, step_rows), step_rows)
+            predicted = (first_sum[at_rows, :] + product(at_rows, HALVES - 1)) * scale
+            aims = targets[t, at_rows, c * size : (c + 1) * size].astype(jnp.float32)
+            pieces = []
+            for q in range(4):
+                present = jnp.zeros((1, size), jnp.int32)
+                for b in range(tile_items):
+                    present = jnp.where(tile_of == b, presence_ref[i * 4 + q, b, ident], present)
+                piece = slice(q * tile_rows, (q + 1) * tile_rows)
+                pieces.append(present.astype(jnp.float32) * (predicted[piece] - aims[piece]))
+            residual = jnp.concatenate(pieces, axis=0).astype(jnp.bfloat16)
+            res[at_rows, c * size : (c + 1) * size] = residual
+            res_t[:, at_rows] = residual.T
+            return carry
+
+        lax.fori_loop(0, n_users // step_rows, predict, 0, unroll=True)
+
+        for h in range(HALVES):
+            part[t, c, h] = (
+                jnp.dot(res_t[...], users_half[:, h * wide : (h + 1) * wide],
+                        preferred_element_type=jnp.float32)
+                * scale
+            ).astype(jnp.bfloat16)
+
+            for copy in part_copies(t, c, h):
+                copy.start()
+
+    def renew(t, c):
+        for h in range(HALVES):
+            part_arrival(t, c, h).wait_recv()
+            own = blk[t, chunk_rows(c, s), columns(h)].astype(jnp.float32)
+            item_grad = part[t, c, h, some(s), :].astype(jnp.float32)
+            for k in range(LINE - 1):
+                item_grad = item_grad + sent[t, c, h, k].astype(jnp.float32)
+            upd[t, c, h] = (own - step_items * (item_grad + decay_weight * own)).astype(
+                jnp.bfloat16
+            )
+            if t < TICKS - 1:
+                for copy in gather_copies(t, c, h):
+                    copy.start()
+            else:
+                final_copy(c, h).start()
+
+    def move_users(t):
+        def body(i, carry):
+            at_rows = pl.ds(pl.multiple_of(i * tall, tall), tall)
+            for q in range(2):
+                part_columns = slice(q * (R // 2), (q + 1) * (R // 2))
+                user_grad = jnp.dot(
+                    res[at_rows, :], blk[t, :, part_columns], preferred_element_type=jnp.float32
+                ) * scale
+                before = users[at_rows, part_columns]
+                after = before - learn_users * (user_grad + decay_weight * before)
+                users[at_rows, part_columns] = after
+                if t < TICKS - 1:
+                    users_half[at_rows, part_columns] = after.astype(jnp.bfloat16)
+            return carry
+
+        lax.fori_loop(0, n_users // tall, body, 0, unroll=2)
+
+    for t in range(TICKS):
+        work(t, 0)
+        if t > 0:
+            renew(t - 1, 1)
+        work(t, 1)
+        renew(t, 0)
+        move_users(t)
+    store_users = pltpu.make_async_copy(users, users_out, local_sem.at[1])
+    store_users.start()
+    renew(TICKS - 1, 1)
+
+    for c in range(CHUNKS):
+        for h in range(HALVES):
+            final_copy(c, h).wait_recv()
+    items_out[...] = final[...]
+    for c in range(CHUNKS):
+        for h in range(HALVES):
+            for copy in first_copies(c, h):
+                copy.wait_send()
+            final_copy(c, h).wait_send()
+            for t in range(TICKS):
+                if t < TICKS - 1:
+                    for copy in gather_copies(t, c, h):
+                        copy.wait_send()
+
+                for copy in part_copies(t, c, h):
+                    copy.wait_send()
+    store_users.wait()
+
+
+def by_line(user_factors, item_factors, ratings, presence, visit_order):
+    n_blk = lax.axis_size("blk")
+    n_users = user_factors.shape[0]
+    part_rows = item_factors.shape[0]
+    rows = part_rows // CHUNKS
+    size = rows * LINE
+    wide = R // HALVES
+    bf16, f32 = jnp.bfloat16, jnp.float32
+    dma = pltpu.SemaphoreType.DMA
+    vmem = pl.BlockSpec(memory_space=pltpu.VMEM)
+    smem = pl.BlockSpec(memory_space=pltpu.SMEM)
+    hbm = pl.BlockSpec(memory_space=pltpu.HBM)
+    flops = 6 * TICKS * n_users * BS * R
+    return pl.pallas_call(
+        functools.partial(line_kernel, n_blk, step_size(LINE * n_users)),
+        out_shape=(
+            jax.ShapeDtypeStruct(user_factors.shape, f32),
+            jax.ShapeDtypeStruct(item_factors.shape, bf16),
+        ),
+        in_specs=[hbm, hbm, hbm, smem, smem],
+        out_specs=(hbm, vmem),
+        scratch_shapes=[
+            pltpu.VMEM((n_users, R), f32),
+            pltpu.VMEM((part_rows, R), bf16),
+            pltpu.VMEM((n_users, R), bf16),
+            pltpu.VMEM(ratings.shape, bf16),
+            pltpu.VMEM((TICKS, n_users, BS), bf16),
+            pltpu.VMEM((n_users, BS), bf16),
+            pltpu.VMEM((size, n_users), bf16),
+            pltpu.VMEM((n_users, size), f32),
+            pltpu.VMEM((TICKS, BS, R), bf16),
+            pltpu.VMEM((TICKS, CHUNKS, HALVES, size, wide), bf16),
+            pltpu.VMEM((TICKS, CHUNKS, HALVES, LINE - 1, rows, wide), bf16),
+            pltpu.VMEM((TICKS, CHUNKS, HALVES, rows, wide), bf16),
+            pltpu.VMEM((part_rows, R), bf16),
+            dma((3,)),
+            dma((TICKS, CHUNKS, HALVES, LINE)),
+            dma((TICKS, CHUNKS, HALVES)),
+            dma((TICKS, CHUNKS, HALVES, LINE - 1)),
+            dma((TICKS, CHUNKS, HALVES)),
+            dma((CHUNKS, HALVES)),
+            dma((CHUNKS, HALVES)),
+        ],
+        compiler_params=pltpu.CompilerParams(
+            collective_id=0, has_side_effects=True, vmem_limit_bytes=56 * 1024 * 1024
+        ),
+        cost_estimate=pl.CostEstimate(
+            flops=flops, bytes_accessed=10 * n_users * R, transcendentals=0
+        ),
+    )(
+        user_factors, item_factors, ratings,
+        jnp.swapaxes(presence, 1, 2), visit_order.reshape(1, -1),
+    )
+
+
 def solution(mesh):
     in_specs = (
         P(("blk", "sub"), None),
@@ -82,6 +381,8 @@
         P(),
     )
     out_specs = (P(("blk", "sub"), None), P(("blk", "sub"), None))
+    lines = mesh.shape["sub"] == LINE and mesh.shape["blk"] > 2
     return jax.shard_map(
-        on_device, mesh=mesh, in_specs=in_specs, out_specs=out_specs, check_vma=False
+        by_line if lines else by_collectives,
+        mesh=mesh, in_specs=in_specs, out_specs=out_specs, check_vma=False,
     )

time: 213 us -> 122 us (0.57)
  Pallas kernels: 0 us -> 114 us
  waiting for transfers between devices: 84.7 us -> 0 us
  blocking collectives: 52.1 us -> 0 us
  matrix products: 30.3 us -> 0 us
  between operations: 21.6 us -> 0.65 us
  starting transfers between devices: 14.3 us -> 0 us
  other arithmetic: 5.3 us -> 0 us
    pallas_call x0 -> x1, Pallas kernels: none -> 114 us  [by_line(): pl.pallas_call(functools.partial(line_kernel, n_blk, step_size(LINE * n_u...]
    reduce_scatter x4 -> x0, waiting for transfers between devices: 82.8 us -> none  [on_device(): lax.psum_scatter(item_part, 'sub', scatter_dimension=0, tiled=True)]
    all_gather x4 -> x0, blocking collectives: 52.1 us -> none  [on_device(): item_block = lax.all_gather(held_part, 'sub', axis=0, tiled=True)]
    dot_general x12 -> x0, matrix products: 30.3 us -> none  [the longest x4 16.6 us: on_device(): jnp.dot(residual, item_block, preferred_element_type=jnp.float32) * scale]
    ppermute x4 -> x0, starting transfers between devices: 14.2 us -> none  [passed_along(): return lax.ppermute(block, axis, route)]
    unnamed x15 -> x4, local copies, waits for them, and re-layouts: 1.05 us -> 5.48 us
    convert_element_type x8 -> x0, other arithmetic: 3.88 us -> none  [the longest x4 3.86 us: on_device(): (own_rows - step_items * (item_grad + decay_weight * own_rows)).astype(jn...]
  transfers between devices with their start and end apart: 8 -> 0, of which waited for: 5 -> 0; matrix products, arithmetic and copies ran while one was open for 8% -> 0% of each run, Pallas kernels for 0% -> 0%
where the time goes in v1:
time: 122 us; the launch traced here: 120 us
  Pallas kernels  114 us (93%)
  local copies, waits for them, and re-layouts  5.48 us (4%)
    pallas_call x1, Pallas kernels, by_line(): pl.pallas_call(functools.partial(line_kernel, n_blk, step_size(LINE * n_u...  114 us
    unnamed x4, local copies, waits for them, and re-layouts  5.48 us

profile of v1, /device:TPU:1, one launch (start us, length us, event | category | flops | bytes accessed | tf_op | source)
XLA Modules:
  0.0 120.0 jit_solution(13356627644789882106)
XLA Ops:
  0.6 113.9 %shard_map.68 = (f32[1024,1024]{1,0:T(8,128)}, bf16[64,1024]{1,0:T(8,128)(2,1)}) custom-call(f32[1024,1024]{1,0:T(8,128)} %users_hbm.1, bf16[64,1024]{1,0:T(8,128)(2,1)} %items_hbm.1, bf16[1024,1024]{1,0:T(8,128)(2,1)} %ratings_hbm.1, s32[8,2,8]{2,1,0:T(2,128)} %bitcast.2, s32[1,8]{1,0:T(1,128)} %bitcast.3), custom_call_target="tpu_custom_call" | custom-call | flops 6442450944 | bytes 10485760 | tf_op jit(solution)/shard_map/pallas_call | solution.py:333
  114.5 0.0 copy-start
  114.5 4.8 %copy.9 = f32[1024,1024]{1,0:T(8,128)} copy(f32[1024,1024]{1,0:T(8,128)} %get-tuple-element.4) | data formatting | bytes 8388608
  119.4 0.0 copy-done
  119.4 0.7 copy.10
Async XLA Ops:
  114.5 4.8 %copy-start = (bf16[64,1024]{1,0:T(8,128)(2,1)S(1)}, bf16[64,1024]{1,0:T(8,128)(2,1)}, u32[]{:S(2)}) copy-start(bf16[64,1024]{1,0:T(8,128)(2,1)} %get-tuple-element.5) | copy-start | bytes 393220
